TPU v7x, 32 devices: a whole 2x2x4 slice. The times are simulated.
32 devices in a mesh: row: 4 (over z), col: 8 (over y, x, core).
Axes of the slice: x: 2, y: 2, z: 4, core: 2. Of those that a mesh axis runs over, the one named last changes fastest.
Arguments:
- tokens: bfloat16 [256, 8192], P('row', 'col'), may hold values from -6 to 6
- gate_weight: bfloat16 [8192, 28672], P('col', 'row'), may hold values from -0.09375 to 0.09375
- up_weight: bfloat16 [8192, 28672], P('col', 'row'), may hold values from -0.09375 to 0.09375
- down_weight: bfloat16 [28672, 8192], P('row', 'col'), may hold values from -0.046875 to 0.046875
- gate_keep: int32 [64, 224], P('col', 'row'), may hold values from 0 to 1, as said below
- up_keep: int32 [64, 224], P('col', 'row'), may hold values from 0 to 1, as said below
- down_keep: int32 [224, 64], P('row', 'col'), may hold values from 0 to 1, as said below
Outputs:
- mixed: bfloat16 [256, 8192], P('row', 'col')
Inputs may be any that keep to these rules, and one draw needn't show every extreme that they name: `gate_keep`: 1 keeps the block, 0 drops it; the kept share differs between regions of blocks. `up_keep`: 1 keeps the block, 0 drops it; the kept share differs between regions of blocks. `down_keep`: 1 keeps the block, 0 drops it; the kept share differs between regions of blocks.
All inputs are finite; a program needn't handle non-finite values.
Results may differ from a plain program's by a relative error of at most 0.0049.
Values may be sent and summed in bfloat16 or wider, within the bound.
A program may use at most 192 MiB of HBM per device.

v0:
```python
import jax
import jax.numpy as jnp
from jax import lax
from jax.sharding import PartitionSpec as P


def expand(weight, keep):
    nrow, ncol = keep.shape
    rows, cols = weight.shape
    masked = (
        weight.reshape(nrow, rows // nrow, ncol, cols // ncol)
        * keep.astype(jnp.bfloat16)[:, None, :, None]
    )
    return masked.reshape(rows, cols)


def on_device(tokens, gate_weight, up_weight, down_weight, gate_keep, up_keep, down_keep):
    paired = jnp.concatenate([expand(gate_weight, gate_keep), expand(up_weight, up_keep)], axis=1)
    down_mat = expand(down_weight, down_keep)
    hidden_cols = gate_weight.shape[1]
    features = lax.all_gather(tokens, "row", axis=0, tiled=True)
    partial_pair = jnp.dot(features, paired, preferred_element_type=jnp.float32)
    summed = lax.psum(partial_pair, "col")
    hidden = (jax.nn.silu(summed[:, :hidden_cols]) * summed[:, hidden_cols:]).astype(jnp.bfloat16)
    partial_out = jnp.dot(hidden, down_mat, preferred_element_type=jnp.float32)
    return lax.psum_scatter(partial_out, "row", scatter_dimension=0, tiled=True).astype(
        jnp.bfloat16
    )


def solution(mesh):
    placed = (
        P("row", "col"),
        P("col", "row"),
        P("col", "row"),
        P("row", "col"),
        P("col", "row"),
        P("col", "row"),
        P("row", "col"),
    )
    return jax.shard_map(
        on_device, mesh=mesh, in_specs=placed, out_specs=P("row", "col"), check_vma=False
    )
```

profile of v0, /device:TPU:0, one launch (start us, length us, event | category | flops | bytes accessed | tf_op | source)
XLA Modules:
  0.0 348.9 jit_solution(18334749804127964281)
XLA Ops:
  6.5 0.0 all-reduce.2.cloned.1.call-start
  6.5 0.7 convert_element_type.15
  7.2 0.7 convert_element_type.16
  7.9 17.6 %all_gather.3 = bf16[256,1024]{1,0:T(8,128)(2,1)S(1)} all-gather(bf16[64,1024]{1,0:T(8,128)(2,1)} %param.7), channel_id=1, replica_groups=mesh['row'=4,'col'=8] {'row'}, dimensions={0}, use_global_device_ids=true | all-gather | bytes 655360 | tf_op jit(solution)/shard_map/all_gather | solution.py:21
  25.5 7.0 %mul.40 = bf16[8,128,56,128]{3,2,1,0:T(8,128)(2,1)} broadcast(bf16[8,56]{1,0:T(8,128)(2,1)S(1)} %convert_element_type.15), dimensions={0,2} | broadcast | bytes 14680960 | tf_op jit(solution)/shard_map/mul | solution.py:11
  32.5 7.2 %mul.43 = bf16[8,128,56,128]{3,2,1,0:T(8,128)(2,1)} broadcast(bf16[8,56]{1,0:T(8,128)(2,1)S(1)} %convert_element_type.16), dimensions={0,2} | broadcast | bytes 14680960 | tf_op jit(solution)/shard_map/mul | solution.py:11
  39.7 30.6 %bitcast_multiply_fusion.2 = (bf16[1024,7168]{1,0:T(8,128)(2,1)}, bf16[1024,7168]{1,0:T(8,128)(2,1)}) fusion(bf16[1024,7168]{1,0:T(8,128)(2,1)} %param.9, bf16[128,8,56,128]{3,2,1,0:T(8,128)(2,1)} %bitcast.17, bf16[1024,7168]{1,0:T(8,128)(2,1)} %param.8, bf16[128,8,56,128]{3,2,1,0:T(8,128)(2,1)} %bitcast.16), kind=kLoop, calls=%fused_computation.8 | loop fusion | flops 14680064 | bytes 88080384 | tf_op jit(solution)/shard_map/mul | solution.py:11
  70.3 21.1 %fusion.4 = f32[256,14336]{0,1:T(8,128)} fusion(bf16[256,1024]{1,0:T(8,128)(2,1)S(1)} %all_gather.3, bf16[1024,7168]{1,0:T(8,128)(2,1)} %get-tuple-element.5, bf16[1024,7168]{1,0:T(8,128)(2,1)} %get-tuple-element.6), kind=kOutput, calls=%fused_computation.4 | convolution fusion | flops 7574913024 | bytes 44564480 | tf_op jit(solution)/shard_map/dot_general | solution.py:22
  91.4 0.0 copy-start
  91.4 0.0 all-reduce.2.cloned.1.call-update
  91.4 0.2 reduce-scatter.2.cloned.1.call-start
  91.6 0.4 copy-done
  92.1 0.1 copy.8
  92.2 196.5 %all-reduce.2.cloned.1.call-done = f32[256,14336]{0,1:T(8,128)} async-done(((f32[256,14336]{0,1:T(8,128)}), f32[256,14336]{0,1:T(8,128)}) %all-reduce.2.cloned.1.call-update) | async-done | bytes 14680080 | tf_op jit(solution)/shard_map/psum | solution.py:23
  288.6 7.1 %mul.48 = bf16[56,128,8,128]{3,2,1,0:T(8,128)(2,1)} broadcast(bf16[56,8]{1,0:T(8,128)(2,1)S(1)} %copy.8), dimensions={0,2} | broadcast | bytes 14680960 | tf_op jit(solution)/shard_map/mul | solution.py:11
  295.8 17.2 %fusion.7 = f32[256,1024]{1,0:T(8,128)} fusion(bf16[7168,1024]{1,0:T(8,128)(2,1)} %param.10, bf16[896,8,8,128]{3,2,1,0:T(8,128)(2,1)} %bitcast.18, f32[256,14336]{0,1:T(8,128)} %all-reduce.2.cloned.1.call-done), kind=kOutput, calls=%fused_computation.6 | convolution fusion | flops 3776446464 | bytes 45088768 | tf_op jit(solution)/shard_map/dot_general | solution.py:25
  313.0 0.0 reduce-scatter.2.cloned.1.call-update
  313.0 27.4 %reduce-scatter.2.cloned.1.call-done = f32[64,1024]{1,0:T(8,128)} async-done(((f32[256,1024]{1,0:T(8,128)}), f32[64,1024]{1,0:T(8,128)}) %reduce-scatter.2.cloned.1.call-update) | async-done | bytes 262160 | tf_op jit(solution)/shard_map/reduce_scatter | solution.py:26
  340.4 1.6 convert_element_type.19
  (1 shorter events, 0.0 us)
Async XLA Ops:
  6.5 282.1 %all-reduce.2.cloned.1.call-start = ((), (), s32[]{:S(2)}) async-start(), calls=%async_computation.1 | async-start | bytes 29360128 | tf_op jit(solution)/shard_map/psum | solution.py:23
  91.4 0.7 copy-start
  91.4 249.1 %reduce-scatter.2.cloned.1.call-start = ((), (), s32[]{:S(2)}) async-start(), calls=%async_computation.2 | async-start | bytes 1310720 | tf_op jit(solution)/shard_map/reduce_scatter | solution.py:26
Sparse Core Ops, SparseCore 0:
  91.5 197.0 all-reduce.1
  313.1 27.2 reduce-scatter.1
where the time goes:
time: 349 us
  waiting for transfers between devices  224 us (64%)
  matrix products  38.3 us (11%)
  other arithmetic  33.6 us (10%)
  local copies, waits for them, and re-layouts  21.9 us (6%)
  blocking collectives  17.6 us (5%)
  between operations  13.4 us (4%)
    psum x1, waiting for transfers between devices, on_device(): summed = lax.psum(partial_pair, 'col')  196 us
    mul x1, other arithmetic, expand(): weight.reshape(nrow, rows // nrow, ncol, cols // ncol)  30.6 us
    reduce_scatter x1, waiting for transfers between devices, on_device(): lax.psum_scatter(partial_out, 'row', scatter_dimension=0, tiled=True)  27.4 us
    mul x3, local copies, waits for them, and re-layouts, expand(): weight.reshape(nrow, rows // nrow, ncol, cols // ncol)  21.3 us
    dot_general x1, matrix products, on_device(): partial_pair = jnp.dot(features, paired, preferred_element_type=jnp.float32)  21.1 us
    all_gather x1, blocking collectives, on_device(): features = lax.all_gather(tokens, 'row', axis=0, tiled=True)  17.6 us
    dot_general x1, matrix products, on_device(): partial_out = jnp.dot(hidden, down_mat, preferred_element_type=jnp.float32)  17.2 us
  transfers between devices with their start and end apart: 2, of which 2 were waited for; matrix products, arithmetic and copies ran while one was open for 0% of the time, Pallas kernels for 0%

commit v1 on v0

v1 whole, which is shorter than its diff:
```python
import functools

import jax
import jax.numpy as jnp
from jax import lax
from jax.experimental import pallas as pl
from jax.experimental.pallas import tpu as pltpu
from jax.sharding import PartitionSpec as P

BLOCK = 128
WIDTH = 512
LAG = 1
SLOTS = 4
MESH = pl.DeviceIdType.MESH


def masked(w, keep_ref, row_block, col_block, nrow, ncol):
    width = ncol * BLOCK
    pieces = []
    for a in range(nrow):
        flags = [
            jnp.full((16, BLOCK), keep_ref[row_block + a, col_block + b].astype(jnp.float32))
            for b in range(ncol)
        ]
        flags = jnp.concatenate(flags, axis=1).astype(jnp.bfloat16)
        rows = w[a * BLOCK : (a + 1) * BLOCK, :].reshape(BLOCK // 16, 16, width)
        pieces.append((rows * flags[None]).reshape(BLOCK, width))
    return jnp.concatenate(pieces, axis=0)


def kernel(rows_n, cols_n, tok_in, gate_w, up_w, down_w, gate_k, up_k, down_k, out, *scratch):
    stages = cols_n.bit_length() - 1
    scratch = list(scratch)
    take = lambda n: [scratch.pop(0) for _ in range(n)]
    tok, gbuf, ubuf, dbuf, part, hid, acc, zsend, zrecv = take(9)
    got = take(stages)
    sent = [None] + take(stages - 1)
    wsem, tsend, trecv, zssem, zrsem, own_sem, rs_send, rs_recv, ag_send, ag_recv = take(10)

    chunks, total, width2 = part.shape
    width = width2 // 2
    local = tok_in.shape[0]
    feats = tok_in.shape[1]
    outs = down_w.shape[1]
    row = lax.axis_index("row")
    col = lax.axis_index("col")
    core = lax.rem(col, 2)

    partner, off, away = [], [0], []
    for j in range(stages):
        if j == 0:
            stride = 1
        else:
            stride = (1 - core) * (1 << j) + core * (1 << (stages - j))
        bit = lax.rem(lax.div(col, stride), 2)
        size = total >> (j + 1)
        partner.append(col + (1 - 2 * bit) * stride)
        away.append(off[j] + (1 - bit) * size)
        off.append(off[j] + bit * size)

    def rows_at(start, size):
        return pl.ds(pl.multiple_of(start, 16), size)

    def weights(c):
        s = lax.rem(c, SLOTS)
        cs = pl.ds(pl.multiple_of(c * width, BLOCK), width)
        return [
            pltpu.make_async_copy(gate_w.at[:, cs], gbuf.at[s], wsem.at[0, s]),
            pltpu.make_async_copy(up_w.at[:, cs], ubuf.at[s], wsem.at[1, s]),
        ]

    def downs(c):
        s = lax.rem(c, SLOTS)
        cs = pl.ds(pl.multiple_of(c * width, BLOCK), width)
        return pltpu.make_async_copy(down_w.at[cs, :], dbuf.at[s], wsem.at[2, s])

    def rs_copy(j, c):
        size = total >> (j + 1)
        src = part.at[c, rows_at(away[0], size)] if j == 0 else sent[j].at[c]
        return pltpu.make_async_remote_copy(
            src_ref=src, dst_ref=got[j].at[c], send_sem=rs_send.at[j, c],
            recv_sem=rs_recv.at[j, c], device_id=(row, partner[j]), device_id_type=MESH,
        )

    def ag_copy(j, c, start):
        view = hid.at[c, rows_at(start, total >> (j + 1))]
        return pltpu.make_async_remote_copy(
            src_ref=view, dst_ref=view, send_sem=ag_send.at[j, c],
            recv_sem=ag_recv.at[j, c], device_id=(row, partner[j]), device_id_type=MESH,
        )

    def tok_copy(i, start):
        return pltpu.make_async_remote_copy(
            src_ref=tok_in, dst_ref=tok.at[rows_at(start, local)], send_sem=tsend.at[i - 1],
            recv_sem=trecv.at[i - 1], device_id=(lax.rem(row + i, rows_n), col),
            device_id_type=MESH,
        )

    def z_copy(i):
        return pltpu.make_async_remote_copy(
            src_ref=zsend.at[i - 1], dst_ref=zrecv.at[i - 1], send_sem=zssem.at[i - 1],
            recv_sem=zrsem.at[i - 1], device_id=(lax.rem(row + i, rows_n), col),
            device_id_type=MESH,
        )

    for c in range(min(SLOTS - 1, chunks)):
        for copy in weights(c):
            copy.start()
        downs(c).start()
    own = pltpu.make_async_copy(tok_in, tok.at[rows_at(row * local, local)], own_sem)
    own.start()

    barrier = pltpu.get_barrier_semaphore()
    for j in range(stages):
        pl.semaphore_signal(barrier, inc=1, device_id=(row, partner[j]), device_id_type=MESH)
    for i in range(1, rows_n):
        pl.semaphore_signal(
            barrier, inc=1, device_id=(lax.rem(row + i, rows_n), col), device_id_type=MESH
        )
    pl.semaphore_wait(barrier, stages + rows_n - 1)

    for i in range(1, rows_n):
        tok_copy(i, row * local).start()
    acc[...] = jnp.zeros_like(acc)
    own.wait()
    for i in range(1, rows_n):
        tok_copy(i, lax.rem(row + rows_n - i, rows_n) * local).wait_recv()

    def expand(c):
        s = lax.rem(c, SLOTS)

        @pl.when(c + SLOTS - 1 < chunks)
        def _():
            for copy in weights(c + SLOTS - 1):
                copy.start()

        nb = width // BLOCK
        for copy, buf, keep, lo in zip(weights(c), (gbuf, ubuf), (gate_k, up_k), (0, width)):
            copy.wait()
            w = masked(buf[s], keep, 0, c * nb, feats // BLOCK, nb)
            part[c, :, lo : lo + width] = jnp.dot(
                tok[...], w, preferred_element_type=jnp.float32
            )
        rs_copy(0, c).start()

    def reduce_step(j, c):
        rs_copy(j, c).wait_recv()
        size = total >> (j + 1)
        if j < stages - 1:
            half = size // 2
            there = rows_at(away[j + 1], half)
            rel = rows_at(away[j + 1] - off[j + 1], half)
            sent[j + 1][c] = (part[c, there] + got[j][c, rel].astype(jnp.float32)).astype(
                jnp.bfloat16
            )
            rs_copy(j + 1, c).start()
            here = rows_at(off[j + 2], half)
            rel = rows_at(off[j + 2] - off[j + 1], half)
            part[c, here] = part[c, here] + got[j][c, rel].astype(jnp.float32)
        else:
            full = part[c, rows_at(off[stages], size)] + got[j][c].astype(jnp.float32)
            gate, up = full[:, :width], full[:, width:]
            hid[c, rows_at(off[stages], size)] = (gate / (1.0 + jnp.exp(-gate)) * up).astype(
                jnp.bfloat16
            )
            ag_copy(j, c, off[stages]).start()

    def gather_step(j, c):
        ag_copy(j, c, away[j]).wait_recv()
        ag_copy(j - 1, c, off[j]).start()

    def contract(c):
        s = lax.rem(c, SLOTS)

        @pl.when(c + SLOTS - 1 < chunks)
        def _():
            downs(c + SLOTS - 1).start()

        ag_copy(0, c, away[0]).wait_recv()
        downs(c).wait()
        nb = width // BLOCK
        w = masked(dbuf[s], down_k, c * nb, 0, nb, outs // BLOCK)
        acc[...] += jnp.dot(hid[c], w, preferred_element_type=jnp.float32)

    depth = 2 * stages
    line = [(LAG * (j + 1), functools.partial(reduce_step, j)) for j in range(stages)]
    line += [
        (LAG * (2 * stages - j), functools.partial(gather_step, j))
        for j in range(stages - 1, 0, -1)
    ]
    line += [(0, expand), (LAG * depth, contract)]

    def step(t, carry):
        for lag, work in line:
            if lag == 0:
                pl.when(t < chunks)(functools.partial(work, t))
            else:
                pl.when((t >= lag) & (t < chunks + lag))(functools.partial(work, t - lag))
        return carry

    lax.fori_loop(0, chunks + LAG * depth, step, 0)

    for i in range(1, rows_n):
        peer = lax.rem(row + i, rows_n)
        zsend[i - 1] = acc[rows_at(peer * local, local)].astype(jnp.bfloat16)
        z_copy(i).start()
    result = acc[rows_at(row * local, local)]
    for i in range(1, rows_n):
        z_copy(i).wait_recv()
        result = result + zrecv[i - 1].astype(jnp.float32)
    out[...] = result.astype(out.dtype)

    def drain(c, carry):
        for j in range(stages):
            rs_copy(j, c).wait_send()
            ag_copy(j, c, off[j + 1]).wait_send()
        return carry

    lax.fori_loop(0, chunks, drain, 0)
    for i in range(1, rows_n):
        tok_copy(i, row * local).wait_send()
        z_copy(i).wait_send()


def on_device(rows_n, cols_n, tokens, gate_w, up_w, down_w, gate_k, up_k, down_k):
    local, feats = tokens.shape
    units = gate_w.shape[1]
    outs = down_w.shape[1]
    total = local * rows_n
    width = min(WIDTH, units)
    chunks = units // width
    stages = cols_n.bit_length() - 1
    bf16, f32 = jnp.bfloat16, jnp.float32
    dma = pltpu.SemaphoreType.DMA
    scratch = [
        pltpu.VMEM((total, feats), bf16),
        pltpu.VMEM((SLOTS, feats, width), bf16),
        pltpu.VMEM((SLOTS, feats, width), bf16),
        pltpu.VMEM((SLOTS, width, outs), bf16),
        pltpu.VMEM((chunks, total, 2 * width), f32),
        pltpu.VMEM((chunks, total, width), bf16),
        pltpu.VMEM((total, outs), f32),
        pltpu.VMEM((rows_n - 1, local, outs), bf16),
        pltpu.VMEM((rows_n - 1, local, outs), bf16),
    ]
    for j in range(stages):
        scratch.append(
            pltpu.VMEM((chunks, total >> (j + 1), 2 * width), f32 if j == 0 else bf16)
        )
    for j in range(1, stages):
        scratch.append(pltpu.VMEM((chunks, total >> (j + 1), 2 * width), bf16))
    scratch += [
        dma((3, SLOTS)),
        dma((rows_n - 1,)),
        dma((rows_n - 1,)),
        dma((rows_n - 1,)),
        dma((rows_n - 1,)),
        dma,
        dma((stages, chunks)),
        dma((stages, chunks)),
        dma((stages, chunks)),
        dma((stages, chunks)),
    ]
    vmem = pl.BlockSpec(memory_space=pltpu.VMEM)
    smem = pl.BlockSpec(memory_space=pltpu.SMEM)
    hbm = pl.BlockSpec(memory_space=pl.ANY)
    flops = 6 * total * feats * units
    return pl.pallas_call(
        functools.partial(kernel, rows_n, cols_n),
        out_shape=jax.ShapeDtypeStruct((local, outs), bf16),
        in_specs=[vmem, hbm, hbm, hbm, smem, smem, smem],
        out_specs=vmem,
        scratch_shapes=scratch,
        compiler_params=pltpu.CompilerParams(
            collective_id=0, has_side_effects=True, vmem_limit_bytes=60 * 1024 * 1024
        ),
        cost_estimate=pl.CostEstimate(
            flops=flops, bytes_accessed=6 * feats * units, transcendentals=0
        ),
        name="swiglu",
    )(tokens, gate_w, up_w, down_w, gate_k, up_k, down_k)


def solution(mesh):
    placed = (
        P("row", "col"),
        P("col", "row"),
        P("col", "row"),
        P("row", "col"),
        P("col", "row"),
        P("col", "row"),
        P("row", "col"),
    )
    return jax.shard_map(
        functools.partial(on_device, mesh.shape["row"], mesh.shape["col"]),
        mesh=mesh, in_specs=placed, out_specs=P("row", "col"), check_vma=False,
    )
```

time: 349 us -> 103 us (0.30)
  waiting for transfers between devices: 224 us -> 0 us
  Pallas kernels: 0 us -> 98.5 us
  matrix products: 38.3 us -> 0 us
  other arithmetic: 33.6 us -> 0 us
  local copies, waits for them, and re-layouts: 21.9 us -> 2.94 us
  blocking collectives: 17.6 us -> 0 us
  between operations: 13.4 us -> 0.01 us
    psum x1 -> x0, waiting for transfers between devices: 196 us -> none  [on_device(): summed = lax.psum(partial_pair, 'col')]
    pallas_call x0 -> x1, Pallas kernels: none -> 98.5 us  [on_device(): pl.pallas_call(functools.partial(kernel, rows_n, cols_n), out_shape=jax.S...]
    dot_general x2 -> x0, matrix products: 38.3 us -> none  [the longest x1 21.1 us: on_device(): partial_pair = jnp.dot(features, paired, preferred_element_type=jnp.float32)]
    mul x1 -> x0, other arithmetic: 30.6 us -> none  [expand(): weight.reshape(nrow, rows // nrow, ncol, cols // ncol)]
    reduce_scatter x1 -> x0, waiting for transfers between devices: 27.4 us -> none  [on_device(): lax.psum_scatter(partial_out, 'row', scatter_dimension=0, tiled=True)]
    mul x3 -> x0, local copies, waits for them, and re-layouts: 21.3 us -> none  [expand(): weight.reshape(nrow, rows // nrow, ncol, cols // ncol)]
    all_gather x1 -> x0, blocking collectives: 17.6 us -> none  [on_device(): features = lax.all_gather(tokens, 'row', axis=0, tiled=True)]
  transfers between devices with their start and end apart: 2 -> 0, of which waited for: 2 -> 0; matrix products, arithmetic and copies ran while one was open for 0% -> 0% of each run, Pallas kernels for 0% -> 0%
where the time goes in v1:
time: 103 us; the launch traced here: 101 us
  Pallas kernels  98.5 us (96%)
  local copies, waits for them, and re-layouts  2.94 us (3%)
    pallas_call x1, Pallas kernels, on_device(): pl.pallas_call(functools.partial(kernel, rows_n, cols_n), out_shape=jax.S...  98.5 us
    unnamed x2, local copies, waits for them, and re-layouts  2.94 us

profile of v1, /device:TPU:0, one launch (start us, length us, event | category | flops | bytes accessed | tf_op | source)
XLA Modules:
  0.0 101.4 jit_solution(953085438861661588)
XLA Ops:
  0.0 1.4 %copy.8.down_k = s32[56,8]{1,0:T(8,128)} copy(s32[56,8]{0,1:T(8,128)} %param.13) | data formatting | bytes 3584 | tf_op args[6]
  1.4 98.5 %swiglu.1 = bf16[64,1024]{1,0:T(8,128)(2,1)} custom-call(bf16[64,1024]{1,0:T(8,128)(2,1)} %tok_in.1, bf16[1024,7168]{1,0:T(8,128)(2,1)} %gate_w.1, bf16[1024,7168]{1,0:T(8,128)(2,1)} %up_w.1, bf16[7168,1024]{1,0:T(8,128)(2,1)} %down_w.1, s32[8,56]{1,0:T(8,128)} %gate_k.1, s32[8,56]{1,0:T(8,128)} %up_k.1, s32[56,8]{1,0:T(8,128)} %copy.8.down_k), custom_call_target="tpu_custom_call" | custom-call | flops 11274289152 | bytes 44040192 | tf_op jit(solution)/shard_map/swiglu/pallas_call | solution.py:268
  99.9 1.6 %copy.10 = bf16[64,1024]{1,0:T(8,128)(2,1)} copy(bf16[64,1024]{1,0:T(8,128)(2,1)} %swiglu.1) | data formatting | bytes 262144

commit v2 on v1

--- a/solution.py
+++ b/solution.py
@@ -8,9 +8,10 @@
 from jax.sharding import PartitionSpec as P
 
 BLOCK = 128
-WIDTH = 512
-LAG = 1
-SLOTS = 4
+WIDTH = 1024
+PASSES = 2
+LAG = 2
+SLOTS = 3
 MESH = pl.DeviceIdType.MESH
 
 
@@ -39,7 +40,8 @@
 
     chunks, total, width2 = part.shape
     width = width2 // 2
-    local = tok_in.shape[0]
+    local = tok_in.shape[0] // PASSES
+    per_pass = chunks // PASSES
     feats = tok_in.shape[1]
     outs = down_w.shape[1]
     row = lax.axis_index("row")
@@ -63,7 +65,7 @@
 
     def weights(c):
         s = lax.rem(c, SLOTS)
-        cs = pl.ds(pl.multiple_of(c * width, BLOCK), width)
+        cs = pl.ds(pl.multiple_of(lax.rem(c, per_pass) * width, BLOCK), width)
         return [
             pltpu.make_async_copy(gate_w.at[:, cs], gbuf.at[s], wsem.at[0, s]),
             pltpu.make_async_copy(up_w.at[:, cs], ubuf.at[s], wsem.at[1, s]),
@@ -71,7 +73,7 @@
 
     def downs(c):
         s = lax.rem(c, SLOTS)
-        cs = pl.ds(pl.multiple_of(c * width, BLOCK), width)
+        cs = pl.ds(pl.multiple_of(lax.rem(c, per_pass) * width, BLOCK), width)
         return pltpu.make_async_copy(down_w.at[cs, :], dbuf.at[s], wsem.at[2, s])
 
     def rs_copy(j, c):
@@ -89,17 +91,18 @@
             recv_sem=ag_recv.at[j, c], device_id=(row, partner[j]), device_id_type=MESH,
         )
 
-    def tok_copy(i, start):
+    def tok_copy(p, i, start):
         return pltpu.make_async_remote_copy(
-            src_ref=tok_in, dst_ref=tok.at[rows_at(start, local)], send_sem=tsend.at[i - 1],
-            recv_sem=trecv.at[i - 1], device_id=(lax.rem(row + i, rows_n), col),
+            src_ref=tok_in.at[p * local : (p + 1) * local],
+            dst_ref=tok.at[p, rows_at(start, local)],
+            send_sem=tsend.at[p, i - 1], recv_sem=trecv.at[p, i - 1], device_id=(lax.rem(row + i, rows_n), col),
             device_id_type=MESH,
         )
 
-    def z_copy(i):
+    def z_copy(p, i):
         return pltpu.make_async_remote_copy(
-            src_ref=zsend.at[i - 1], dst_ref=zrecv.at[i - 1], send_sem=zssem.at[i - 1],
-            recv_sem=zrsem.at[i - 1], device_id=(lax.rem(row + i, rows_n), col),
+            src_ref=zsend.at[p, i - 1], dst_ref=zrecv.at[p, i - 1], send_sem=zssem.at[p, i - 1],
+            recv_sem=zrsem.at[p, i - 1], device_id=(lax.rem(row + i, rows_n), col),
             device_id_type=MESH,
         )
 
@@ -107,8 +110,16 @@
         for copy in weights(c):
             copy.start()
         downs(c).start()
-    own = pltpu.make_async_copy(tok_in, tok.at[rows_at(row * local, local)], own_sem)
-    own.start()
+    own = [
+        pltpu.make_async_copy(
+            tok_in.at[p * local : (p + 1) * local],
+            tok.at[p, rows_at(row * local, local)],
+            own_sem.at[p],
+        )
+        for p in range(PASSES)
+    ]
+    for copy in own:
+        copy.start()
 
     barrier = pltpu.get_barrier_semaphore()
     for j in range(stages):
@@ -119,12 +130,25 @@
         )
     pl.semaphore_wait(barrier, stages + rows_n - 1)
 
+    def tokens_in(p):
+        for i in range(1, rows_n):
+            tok_copy(p, i, lax.rem(row + rows_n - i, rows_n) * local).wait_recv()
+        if p + 1 < PASSES:
+            for i in range(1, rows_n):
+                tok_copy(p + 1, i, row * local).start()
+
     for i in range(1, rows_n):
-        tok_copy(i, row * local).start()
+        tok_copy(0, i, row * local).start()
     acc[...] = jnp.zeros_like(acc)
-    own.wait()
-    for i in range(1, rows_n):
-        tok_copy(i, lax.rem(row + rows_n - i, rows_n) * local).wait_recv()
+    for copy in own:
+        copy.wait()
+    tokens_in(0)
+
+    def results_out(p):
+        for i in range(1, rows_n):
+            peer = lax.rem(row + i, rows_n)
+            zsend[p, i - 1] = acc[p, rows_at(peer * local, local)].astype(jnp.bfloat16)
+            z_copy(p, i).start()
 
     def expand(c):
         s = lax.rem(c, SLOTS)
@@ -134,12 +158,16 @@
             for copy in weights(c + SLOTS - 1):
                 copy.start()
 
+        for p in range(1, PASSES):
+            pl.when(c == p * per_pass)(functools.partial(tokens_in, p))
+
         nb = width // BLOCK
+        first = lax.rem(c, per_pass) * nb
         for copy, buf, keep, lo in zip(weights(c), (gbuf, ubuf), (gate_k, up_k), (0, width)):
             copy.wait()
-            w = masked(buf[s], keep, 0, c * nb, feats // BLOCK, nb)
+            w = masked(buf[s], keep, 0, first, feats // BLOCK, nb)
             part[c, :, lo : lo + width] = jnp.dot(
-                tok[...], w, preferred_element_type=jnp.float32
+                tok[lax.div(c, per_pass)], w, preferred_element_type=jnp.float32
             )
         rs_copy(0, c).start()
 
@@ -179,8 +207,11 @@
         ag_copy(0, c, away[0]).wait_recv()
         downs(c).wait()
         nb = width // BLOCK
-        w = masked(dbuf[s], down_k, c * nb, 0, nb, outs // BLOCK)
-        acc[...] += jnp.dot(hid[c], w, preferred_element_type=jnp.float32)
+        w = masked(dbuf[s], down_k, lax.rem(c, per_pass) * nb, 0, nb, outs // BLOCK)
+        now = lax.div(c, per_pass)
+        acc[now] = acc[now] + jnp.dot(hid[c], w, preferred_element_type=jnp.float32)
+        for p in range(PASSES):
+            pl.when(c == (p + 1) * per_pass - 1)(functools.partial(results_out, p))
 
     depth = 2 * stages
     line = [(LAG * (j + 1), functools.partial(reduce_step, j)) for j in range(stages)]
@@ -200,15 +231,12 @@
 
     lax.fori_loop(0, chunks + LAG * depth, step, 0)
 
-    for i in range(1, rows_n):
-        peer = lax.rem(row + i, rows_n)
-        zsend[i - 1] = acc[rows_at(peer * local, local)].astype(jnp.bfloat16)
-        z_copy(i).start()
-    result = acc[rows_at(row * local, local)]
-    for i in range(1, rows_n):
-        z_copy(i).wait_recv()
-        result = result + zrecv[i - 1].astype(jnp.float32)
-    out[...] = result.astype(out.dtype)
+    for p in range(PASSES):
+        result = acc[p, rows_at(row * local, local)]
+        for i in range(1, rows_n):
+            z_copy(p, i).wait_recv()
+            result = result + zrecv[p, i - 1].astype(jnp.float32)
+        out[p * local : (p + 1) * local] = result.astype(out.dtype)
 
     def drain(c, carry):
         for j in range(stages):
@@ -217,31 +245,33 @@
         return carry
 
     lax.fori_loop(0, chunks, drain, 0)
-    for i in range(1, rows_n):
-        tok_copy(i, row * local).wait_send()
-        z_copy(i).wait_send()
+    for p in range(PASSES):
+        for i in range(1, rows_n):
+            tok_copy(p, i, row * local).wait_send()
+            z_copy(p, i).wait_send()
 
 
 def on_device(rows_n, cols_n, tokens, gate_w, up_w, down_w, gate_k, up_k, down_k):
     local, feats = tokens.shape
     units = gate_w.shape[1]
     outs = down_w.shape[1]
+    local = local // PASSES
     total = local * rows_n
-    width = min(WIDTH, units)
-    chunks = units // width
+    width = next(w for w in range(WIDTH, 0, -BLOCK) if units % w == 0)
+    chunks = PASSES * (units // width)
     stages = cols_n.bit_length() - 1
     bf16, f32 = jnp.bfloat16, jnp.float32
     dma = pltpu.SemaphoreType.DMA
     scratch = [
-        pltpu.VMEM((total, feats), bf16),
+        pltpu.VMEM((PASSES, total, feats), bf16),
         pltpu.VMEM((SLOTS, feats, width), bf16),
         pltpu.VMEM((SLOTS, feats, width), bf16),
         pltpu.VMEM((SLOTS, width, outs), bf16),
         pltpu.VMEM((chunks, total, 2 * width), f32),
         pltpu.VMEM((chunks, total, width), bf16),
-        pltpu.VMEM((total, outs), f32),
-        pltpu.VMEM((rows_n - 1, local, outs), bf16),
-        pltpu.VMEM((rows_n - 1, local, outs), bf16),
+        pltpu.VMEM((PASSES, total, outs), f32),
+        pltpu.VMEM((PASSES, rows_n - 1, local, outs), bf16),
+        pltpu.VMEM((PASSES, rows_n - 1, local, outs), bf16),
     ]
     for j in range(stages):
         scratch.append(
@@ -251,11 +281,11 @@
         scratch.append(pltpu.VMEM((chunks, total >> (j + 1), 2 * width), bf16))
     scratch += [
         dma((3, SLOTS)),
-        dma((rows_n - 1,)),
-        dma((rows_n - 1,)),
-        dma((rows_n - 1,)),
-        dma((rows_n - 1,)),
-        dma,
+        dma((PASSES, rows_n - 1)),
+        dma((PASSES, rows_n - 1)),
+        dma((PASSES, rows_n - 1)),
+        dma((PASSES, rows_n - 1)),
+        dma((PASSES,)),
         dma((stages, chunks)),
         dma((stages, chunks)),
         dma((stages, chunks)),
@@ -264,10 +294,10 @@
     vmem = pl.BlockSpec(memory_space=pltpu.VMEM)
     smem = pl.BlockSpec(memory_space=pltpu.SMEM)
     hbm = pl.BlockSpec(memory_space=pl.ANY)
-    flops = 6 * total * feats * units
+    flops = 6 * PASSES * total * feats * units
     return pl.pallas_call(
         functools.partial(kernel, rows_n, cols_n),
-        out_shape=jax.ShapeDtypeStruct((local, outs), bf16),
+        out_shape=jax.ShapeDtypeStruct((PASSES * local, outs), bf16),
         in_specs=[vmem, hbm, hbm, hbm, smem, smem, smem],
         out_specs=vmem,
         scratch_shapes=scratch,

time: 103 us -> 79.1 us (0.77); the launches traced: 101 us -> 78.9 us
  Pallas kernels: 98.5 us -> 75.9 us
    pallas_call x1, Pallas kernels: 98.5 us -> 75.9 us  [on_device(): pl.pallas_call(functools.partial(kernel, rows_n, cols_n), out_shape=jax.S...]
where the time goes in v2:
time: 79.1 us; the launch traced here: 78.9 us
  Pallas kernels  75.9 us (96%)
  local copies, waits for them, and re-layouts  2.94 us (4%)
    pallas_call x1, Pallas kernels, on_device(): pl.pallas_call(functools.partial(kernel, rows_n, cols_n), out_shape=jax.S...  75.9 us
    unnamed x2, local copies, waits for them, and re-layouts  2.94 us

profile of v2, /device:TPU:0, one launch (start us, length us, event | category | flops | bytes accessed | tf_op | source)
XLA Modules:
  0.0 78.9 jit_solution(9448155076102050568)
XLA Ops:
  0.0 1.4 %copy.8.down_k = s32[56,8]{1,0:T(8,128)} copy(s32[56,8]{0,1:T(8,128)} %param.13) | data formatting | bytes 3584 | tf_op args[6]
  1.4 75.9 %swiglu.1 = bf16[64,1024]{1,0:T(8,128)(2,1)} custom-call(bf16[64,1024]{1,0:T(8,128)(2,1)} %tok_in.1, bf16[1024,7168]{1,0:T(8,128)(2,1)} %gate_w.1, bf16[1024,7168]{1,0:T(8,128)(2,1)} %up_w.1, bf16[7168,1024]{1,0:T(8,128)(2,1)} %down_w.1, s32[8,56]{1,0:T(8,128)} %gate_k.1, s32[8,56]{1,0:T(8,128)} %up_k.1, s32[56,8]{1,0:T(8,128)} %copy.8.down_k), custom_call_target="tpu_custom_call" | custom-call | flops 11274289152 | bytes 44040192 | tf_op jit(solution)/shard_map/swiglu/pallas_call | solution.py:298
  77.3 1.6 %copy.10 = bf16[64,1024]{1,0:T(8,128)(2,1)} copy(bf16[64,1024]{1,0:T(8,128)(2,1)} %swiglu.1) | data formatting | bytes 262144
